TPU v7x, 32 devices: a whole 2x2x4 slice. The times are simulated.
32 devices in a mesh: groups: 2 (over y), seq: 8 (over z, x), batch: 2 (over core).
Axes of the slice: x: 2, y: 2, z: 4, core: 2. Of those that a mesh axis runs over, the one named last changes fastest.
Arguments:
- tokens: int32 [4, 4096], P(('groups', 'batch'), 'seq'), parts along dimension 0, may hold values from 0 to 3
- hidden: bfloat16 [4, 4096, 1024], P(('groups', 'batch'), 'seq'), parts along dimension 0, may hold values from -6 to 6
- base_table: bfloat16 [4, 1024], replicated, may hold values from -6 to 6
- w_in: bfloat16 [1024, 2304], replicated, may hold values from -0.1875 to 0.1875
- w_dt: bfloat16 [1024, 16], replicated, may hold values from -0.1875 to 0.1875
- conv_w: float32 [4, 1280], replicated, may hold values from -3 to 3
- conv_b: float32 [1280], replicated, may hold values from -3 to 3
- dt_bias: float32 [16], replicated, as said below
- a_log: float32 [16], replicated, as said below
- d_skip: float32 [16], replicated, may hold values from 0.5 to 1.5
- norm_gain: float32 [1024], replicated, may hold values from 0.1 to 1.9
- w_out: bfloat16 [1024, 1024], replicated, may hold values from -0.1875 to 0.1875
Outputs:
- mixed: bfloat16 [4, 4096, 1024], P(('groups', 'batch'), 'seq'), parts along dimension 0
There are 2 independent parts, one for each index of `groups`. A program takes and returns all parts, laid end to end along the dimension named above; an argument that names none is the same for every part. Nothing has to cross between parts.
Inputs may be any that keep to these rules, and one draw needn't show every extreme that they name: `a_log`: real numbers, one for each head. `dt_bias`: real numbers, one for each head.
All inputs are finite; a program needn't handle non-finite values.
Results may differ from a plain program's by a relative error of at most 0.0017.
The roundings to bfloat16 on the way count: a program that leaves them out, or rounds other values in their place, can miss the bound.
Values may be sent and summed in bfloat16 or wider, within the bound.
A program may use at most 192 MiB of HBM per device.

v0:
```python
from functools import partial

import jax
import jax.numpy as jnp
from jax import lax
from jax.sharding import PartitionSpec as P

H = 16
P_SIZE = 64
N = 128
Q = 256
KCONV = 4


norm_epsilon = 1e-05


def padded(block, sides, width):
    for axis, dim in sides:
        count = lax.axis_size(axis)
        forward = [(i, i + 1) for i in range(count - 1)]
        backward = [(target, source) for source, target in forward]
        low = lax.ppermute(
            lax.slice_in_dim(block, block.shape[dim] - width, None, axis=dim), axis, forward
        )
        high = lax.ppermute(lax.slice_in_dim(block, 0, width, axis=dim), axis, backward)
        block = jnp.concatenate([low, block, high], axis=dim)
    return block


def prefix(part, axis, combine, identity, reverse):
    count = lax.axis_size(axis)
    place = lax.axis_index(axis)
    ahead = count - 1 - place if reverse else place
    gathered = jax.tree.map(lambda a: lax.all_gather(a, axis), part)
    state = jax.tree.map(lambda a, e: jnp.zeros_like(a) + jnp.asarray(e, a.dtype), part, identity)

    def one(hop, state):
        source = count - 1 - hop if reverse else hop
        return combine(
            state, jax.tree.map(lambda a: lax.dynamic_index_in_dim(a, source, 0, False), gathered)
        )

    return lax.fori_loop(0, ahead, one, state)


def span_terms(heads_x, b_rows, c_rows, step_size, rates):
    log_decay = jnp.cumsum(step_size * rates[None, :], axis=0)
    across = jnp.transpose(log_decay)
    width = across.shape[1]
    lower = (jnp.arange(width)[:, None] >= jnp.arange(width)[None, :])[None]
    gaps = across[:, :, None] - across[:, None, :]
    decays = jnp.where(lower, jnp.exp(jnp.where(lower, gaps, 0.0)), 0.0)
    scores = jnp.dot(c_rows, jnp.transpose(b_rows), preferred_element_type=jnp.float32)
    weights = (decays * scores[None] * jnp.transpose(step_size)[:, None, :]).astype(jnp.bfloat16)
    inside = jnp.einsum("hts,shp->thp", weights, heads_x, preferred_element_type=jnp.float32)
    to_end = jnp.exp(log_decay[-1][None, :] - log_decay) * step_size
    state_weights = (b_rows.astype(jnp.float32)[:, None, :] * to_end[:, :, None]).astype(
        jnp.bfloat16
    )
    state = jnp.einsum("shp,shn->hpn", heads_x, state_weights, preferred_element_type=jnp.float32)
    return (inside, state, jnp.exp(log_decay[-1]), jnp.exp(log_decay))


def local_terms(extended, w_in, w_dt, conv_w, conv_b, dt_bias, a_log):
    inner = H * P_SIZE
    margin = KCONV - 1
    rows_here = extended.shape[1] - margin
    count = extended.shape[0]
    projected = jnp.einsum("grd,de->gre", extended, w_in, preferred_element_type=jnp.float32)
    source = projected[:, :, inner:]
    summed = jnp.broadcast_to(conv_b, (count, rows_here, conv_b.shape[0]))
    for tap in range(KCONV):
        summed = summed + conv_w[tap] * source[:, tap : tap + rows_here]
    activated = jax.nn.silu(summed).astype(jnp.bfloat16)
    step_size = jax.nn.softplus(
        jnp.einsum("grd,dh->grh", extended[:, margin:], w_dt, preferred_element_type=jnp.float32)
        + dt_bias
    )
    spans = rows_here // Q
    heads_x = activated[:, :, :inner].reshape(count, spans, Q, H, P_SIZE)
    b_rows = activated[:, :, inner : inner + N].reshape(count, spans, Q, N)
    c_rows = activated[:, :, inner + N :].reshape(count, spans, Q, N)
    steps_cut = step_size.reshape(count, spans, Q, H)
    rates = -jnp.exp(a_log)
    per_span = jax.vmap(jax.vmap(partial(span_terms, rates=rates)))
    inside, state, total, from_start = per_span(heads_x, b_rows, c_rows, steps_cut)

    def advance(carry, pieces):
        decay_sofar, state_sofar = carry
        total_here, state_here = pieces
        updated = (
            decay_sofar * total_here,
            total_here[:, :, None, None] * state_sofar + state_here,
        )
        return (updated, (decay_sofar, state_sofar))

    start = (jnp.ones((count, H), jnp.float32), jnp.zeros((count, H, P_SIZE, N), jnp.float32))
    summary, before = lax.scan(
        advance, start, (jnp.moveaxis(total, 1, 0), jnp.moveaxis(state, 1, 0))
    )
    gate_part = projected[:, margin:, :inner]
    return (summary, (before, inside, from_start, heads_x, c_rows, gate_part))


def normalize(pending, incoming, d_skip, norm_gain):
    before, inside, from_start, heads_x, c_rows, gate_part = pending
    before_decay, before_state = before
    start_state = before_state + before_decay[:, :, :, None, None] * incoming[None]
    start_state = jnp.moveaxis(start_state, 0, 1)
    carried = jnp.einsum(
        "gctn,gchpn->gcthp",
        c_rows.astype(jnp.float32),
        start_state,
        precision=lax.Precision.HIGHEST,
    )
    scanned = (
        inside + from_start[..., None] * carried + d_skip[:, None] * heads_x.astype(jnp.float32)
    )
    count = scanned.shape[0]
    flat = scanned.reshape(count, -1, H * P_SIZE)
    gated = flat * jax.nn.silu(gate_part)
    return (
        gated
        * lax.rsqrt(jnp.mean(gated * gated, axis=-1, keepdims=True) + norm_epsilon)
        * norm_gain
    ).astype(jnp.bfloat16)


def project(normed, w_out):
    return jnp.einsum("grk,kd->grd", normed, w_out, preferred_element_type=jnp.float32)


def chain_states(earlier, later):
    first_decay, first_state = earlier
    next_decay, next_state = later
    return (first_decay * next_decay, next_decay[..., None, None] * first_state + next_state)


def on_device(
    tokens, hidden, base_table, w_in, w_dt, conv_w, conv_b, dt_bias, a_log, d_skip, norm_gain, w_out
):
    slabs = hidden.shape[0]
    rows_here = hidden.shape[1]
    margin = KCONV - 1
    one_hot = (tokens[:, :, None] == jnp.arange(4)[None, None, :]).astype(jnp.bfloat16)
    looked = jnp.einsum("gtb,bd->gtd", one_hot, base_table, preferred_element_type=jnp.float32)
    strand_input = (hidden.astype(jnp.float32) + looked).astype(jnp.bfloat16)
    extended_all = padded(strand_input, (("seq", 1),), margin)
    forward_ext = extended_all[:, : rows_here + margin]
    reverse_ext = extended_all[:, margin:][:, ::-1, ::-1]
    extended = jnp.concatenate([forward_ext, reverse_ext], axis=0)
    summary, pending = local_terms(extended, w_in, w_dt, conv_w, conv_b, dt_bias, a_log)
    sum_decay, sum_state = summary
    neutral = (jnp.ones((slabs, H), jnp.float32), jnp.zeros((slabs, H, P_SIZE, N), jnp.float32))
    forward_in = prefix((sum_decay[:slabs], sum_state[:slabs]), "seq", chain_states, neutral, False)
    reverse_in = prefix((sum_decay[slabs:], sum_state[slabs:]), "seq", chain_states, neutral, True)
    incoming_state = jnp.concatenate([forward_in[1], reverse_in[1]], axis=0)
    outputs = project(normalize(pending, incoming_state, d_skip, norm_gain), w_out)
    mixed = outputs[:slabs] + outputs[slabs:][:, ::-1, ::-1]
    return mixed.astype(jnp.bfloat16)


def solution(mesh):
    placed = (
        P(("groups", "batch"), "seq"),
        P(("groups", "batch"), "seq", None),
        P(),
        P(),
        P(),
        P(),
        P(),
        P(),
        P(),
        P(),
        P(),
        P(),
    )
    return jax.shard_map(
        on_device,
        mesh=mesh,
        in_specs=placed,
        out_specs=P(("groups", "batch"), "seq", None),
        check_vma=False,
    )
```

profile of v0, /device:TPU:0, one launch (start us, length us, event | category | flops | bytes accessed | tf_op | source)
XLA Modules:
  0.0 314.3 jit_solution(1577532329183253447)
XLA Ops:
  6.5 1.9 fusion.32
  8.4 1.0 copy-done.3
  9.4 1.3 collective-permute-start.1
  10.7 5.5 %collective-permute-start = (bf16[1,3,1024]{2,1,0:T(4,128)(2,1)S(1)}, bf16[1,3,1024]{2,1,0:T(4,128)(2,1)S(1)}, u32[]{:S(2)}, u32[]{:S(2)}) collective-permute-start(bf16[1,3,1024]{2,1,0:T(4,128)(2,1)S(1)} %get-tuple-element.313), channel_id=1, source_target_pairs={{0,2},{2,4},{4,6},{6,8},{8,10},{10,12},{12,14},{1,3},{3,5},{5,7},{... | collective-permute-start | bytes 18440 | tf_op jit(solution)/shard_map/ppermute | solution.py:23
  16.9 0.9 slice_reduce_fusion.5
  17.8 2.3 pad_maximum_fusion
  20.1 20.6 %rev.6 = bf16[1,515,1024]{2,1,0:T(8,128)(2,1)} reverse(bf16[1,515,1024]{2,1,0:T(8,128)(2,1)} %pad_maximum_fusion), dimensions={1,2} | reverse | bytes 2109440 | tf_op jit(solution)/shard_map/rev | solution.py:151
  40.7 8.2 %fusion.12 = f32[2,515,2304]{2,1,0:T(8,128)S(1)} fusion(bf16[1024,2304]{1,0:T(8,128)(2,1)} %param.21, bf16[1,515,1024]{2,1,0:T(8,128)(2,1)} %rev.6, bf16[1,512,1024]{2,1,0:T(8,128)(2,1)} %copy-done.3, bf16[1,3,1024]{2,1,0:T(4,128)(2,1)S(1)} %collective-permute-done), kind=kOutput, calls=%fused_computation.28 | convolution fusion | flops 4866478080 | bytes 16320512 | tf_op jit(solution)/shard_map/grd,de->gre/dot_general | solution.py:70
  49.0 3.4 %multiply_convert_fusion.3 = bf16[2,512,1280]{2,1,0:T(8,128)(2,1)S(1)} fusion(f32[2,515,2304]{2,1,0:T(8,128)S(1)} %fusion.12, f32[1280]{0:T(1024)S(1)} %get-tuple-element.273, f32[1280]{0:T(1024)S(1)} %get-tuple-element.274, f32[1280]{0:T(1024)S(1)} %get-tuple-element.272, f32[1280]{0:T(1024)S(1)} %get-tuple-element.271, f32[1280]{0:T(1024)S(1)} %copy-done.13), kind=kLoop, calls=%fused_computation.27 | loop fusion | flops 17039360 | bytes 23618560 | tf_op jit(solution)/shard_map/convert_element_type | solution.py:75
  52.6 0.8 fusion.50
  53.5 1.6 slice.112
  55.8 0.7 copy_bitcast_fusion.1
  56.5 4.2 %reduce-window.6 = f32[2,2,16,2,128]{4,2,3,1,0:T(8,128)S(1)} reduce-window(f32[2,2,16,2,128]{4,2,3,1,0:T(8,128)} %copy_bitcast_fusion.1, f32[]{:T(128)} %constant.86.clone.1), window={size=1x1x1x1x128 pad=0_0x0_0x0_0x0_0x127_0}, to_apply=%region_0.1 | reduce-window | flops 2080768 | bytes 131076 | tf_op jit(solution)/shard_map/reduce-window
  60.9 0.7 copy_bitcast_fusion
  61.7 0.8 bitcast_exponential_fusion
  62.5 1.8 convert_element_type.37
  64.3 6.4 %reshape.127 = bf16[2,2,256,16,64]{4,3,2,1,0:T(8,128)(2,1)} reshape(bf16[2,512,1024]{2,1,0:T(8,128)(2,1)} %slice.112) | data formatting | bytes 4194304 | tf_op jit(solution)/shard_map/reshape | solution.py:81
  70.7 5.8 %copy.65 = bf16[2,2,256,16,64]{2,4,3,1,0:T(8,128)(2,1)} copy(bf16[2,2,256,16,64]{4,3,2,1,0:T(8,128)(2,1)} %reshape.127) | data formatting | bytes 4194304 | tf_op jit(solution)/shard_map/reshape | solution.py:81
  76.5 5.1 %fusion.37 = f32[2,2,16,64,128]{4,3,2,0,1:T(8,128)} fusion(bf16[2,2,256,16,64]{2,4,3,1,0:T(8,128)(2,1)} %copy.65, f32[2,2,256,16]{2,3,1,0:T(8,128)S(1)} %copy-done.12, f32[2,2,256,128]{3,2,1,0:T(8,128)} %convert_element_type.37), kind=kOutput, calls=%fused_computation.60 | convolution fusion | flops 272629760 | bytes 4784128 | tf_op jit(solution)/shard_map/vmap(vmap(shp,shn->hpn))/dot_general | solution.py:61
  81.7 5.0 %while.45 = (s32[]{:T(128)}, f32[2,16]{1,0:T(2,128)S(1)}, f32[2,16,64,128]{3,2,1,0:T(8,128)S(1)}, f32[2,2,16]{2,1,0:T(2,128)S(1)}, f32[2,2,16,64,128]{4,3,2,1,0:...) while((s32[]{:T(128)}, f32[2,16]{1,0:T(2,128)S(1)}, ...), condition=%wide.region_3.4_spmd.clone, body=%wide.region_2.3_spmd.clone.sunk | while | flops 1048675 | bytes 5246326 | solution.py:99
  81.7 1.1 bitcast_dynamic-update-slice_fusion.5
  82.7 1.4 bitcast_add_fusion.10
  84.2 1.0 bitcast_dynamic-update-slice_fusion.5
  85.2 1.4 bitcast_add_fusion.10
  86.7 1.1 fusion.51
  89.3 19.4 %all-gather.4 = f32[8,1,16]{2,1,0:T(1,128)S(1)} all-gather(f32[1,1,16]{2,1,0:T(1,128)S(1)} %get-tuple-element.319), channel_id=2, replica_groups=mesh['groups'=2,'seq'=8,'batch'=2] {'seq'}, dimensions={0}, use_global_device_ids=true | all-gather | bytes 576 | tf_op jit(solution)/shard_map/all_gather | solution.py:35
  108.7 16.3 %all-gather.5 = f32[8,1,16]{2,1,0:T(1,128)S(1)} all-gather(f32[1,1,16]{2,1,0:T(1,128)S(1)} %get-tuple-element.320), channel_id=4, replica_groups=mesh['groups'=2,'seq'=8,'batch'=2] {'seq'}, dimensions={0}, use_global_device_ids=true | all-gather | bytes 576 | tf_op jit(solution)/shard_map/all_gather | solution.py:35
  125.0 2.2 fusion.53
  127.2 35.9 %all-gather.9.cloned.1.call-done = f32[8,16,64,128]{3,2,1,0:T(8,128)} async-done(((f32[1,16,64,128]{3,2,1,0:T(8,128)}), f32[8,16,64,128]{3,2,1,0:T(8,128)}) %all-gather.9.cloned.1.call-update) | async-done | bytes 4194320 | tf_op jit(solution)/shard_map/all_gather | solution.py:35
  163.2 73.8 %all-gather.11.cloned.1.call-done = f32[8,16,64,128]{3,2,1,0:T(8,128)} async-done(((f32[1,16,64,128]{3,2,1,0:T(8,128)}), f32[8,16,64,128]{3,2,1,0:T(8,128)}) %all-gather.11.cloned.1.call-update) | async-done | bytes 4194320 | tf_op jit(solution)/shard_map/all_gather | solution.py:35
  237.0 8.8 %while.44 = (s32[]{:T(128)}, f32[1,16,64,128]{3,2,1,0:T(8,128)S(1)}, s32[]{:T(128)}, f32[8,1,16]{2,1,0:T(1,128)S(1)}, f32[8,1,16,64,128]{4,3,2,1,0:T(8,128)}, /*index=5*/s32[]{:T(128)}, s32[]{:T(128)}, s32[]{:T(128)}, s32[]{:T(128)}) while((s32[]{:T(128)}, f32[1,16,64,128]{3,2,1,0:T(8,128)S(1)}, s32[]{:T(128)}, f32[8,1,16]{2,1,0:T(1,128)S(1)}, ...), condition=%wide.region_7.8_spmd, body=%wide.region_6.7_spmd.sunk | while | flops 262150 | bytes 1573203 | solution.py:44
  237.0 1.2 bitcast_add_fusion.9
  238.2 1.2 bitcast_add_fusion.9
  239.5 1.2 bitcast_add_fusion.9
  240.7 1.2 bitcast_add_fusion.9
  241.9 1.2 bitcast_add_fusion.9
  243.2 1.2 bitcast_add_fusion.9
  244.4 1.2 bitcast_add_fusion.9
  245.9 3.7 %fusion.33 = f32[2,2,256,16,64]{2,4,3,1,0:T(8,128)S(1)} fusion(bf16[2,2,256,128,1]{3,2,4,1,0:T(8,128)(2,1)S(1)} %bitcast.118, f32[2,2,16,64,128]{4,3,2,1,0:T(8,128)} %get-tuple-element.173, f32[2,16,64,128]{3,2,1,0:T(8,128)S(1)} %pad_maximum_fusion.1, f32[2,2,16]{2,1,0:T(2,128)S(1)} %get-tuple-element.174), kind=kOutput, calls=%fused_computation.55 | convolution fusion | flops 1611661312 | bytes 7602432 | tf_op jit(solution)/shard_map/gctn,gchpn->gcthp/dot_general | solution.py:111
  249.7 7.1 %fusion.15 = f32[2,2,256,16,64]{2,4,3,1,0:T(8,128)} fusion(bf16[2,2,256,16,64]{2,4,3,1,0:T(8,128)(2,1)S(1)} %copy-done.6, f32[2,2,256,16,64]{2,4,3,1,0:T(8,128)S(1)} %fusion.33, f32[2,2,16,256]{3,2,1,0:T(8,128)S(1)} %copy.64, f32[2,2,256,256]{3,2,1,0:T(8,128)S(1)} %copy-done.8, f32[2,2,16,256]{3,2,1,0:T(8,128)S(1)} %copy-done.9, ...), kind=kOutput, calls=%fused_computation.32 | convolution fusion | flops 567279616 | bytes 11796544 | tf_op jit(solution)/shard_map/vmap(vmap(hts,shp->thp))/dot_general | solution.py:56
  256.8 8.1 %copy.77 = f32[2,2,256,16,64]{4,3,2,1,0:T(8,128)} copy(f32[2,2,256,16,64]{2,4,3,1,0:T(8,128)} %fusion.15) | data formatting | bytes 8388608 | tf_op jit(solution)/shard_map/reshape | solution.py:121
  264.9 7.6 %reshape.126 = f32[2,512,1024]{2,1,0:T(8,128)} reshape(f32[2,2,256,16,64]{4,3,2,1,0:T(8,128)} %copy.77) | data formatting | bytes 8388608 | tf_op jit(solution)/shard_map/reshape | solution.py:121
  272.5 5.1 %multiply_reduce_fusion = f32[2,512]{1,0:T(2,128)S(1)} fusion(f32[2,512,1024]{2,1,0:T(8,128)} %reshape.126, f32[2,515,2304]{2,1,0:T(8,128)} %copy-done.1), kind=kLoop, calls=%fused_computation.34 | loop fusion | flops 7339008 | bytes 8392704 | tf_op jit(solution)/shard_map/reduce_sum | solution.py:125
  277.6 5.1 %fusion.23 = f32[2,512,1024]{2,1,0:T(8,128)S(1)} fusion(bf16[1024,1024]{1,0:T(8,128)(2,1)S(1)} %copy-done, f32[1024]{0:T(1024)S(1)} %copy-done.16, f32[2,512]{1,0:T(2,128)S(1)} %add_rsqrt_fusion, f32[2,512,1024]{2,1,0:T(8,128)S(1)} %copy-done.2, f32[2,515,2304]{2,1,0:T(8,128)} %copy-done.1), kind=kOutput, calls=%fused_computation.43 | convolution fusion | flops 2155872256 | bytes 14688256 | tf_op jit(solution)/shard_map/grk,kd->grd/dot_general | solution.py:131
  282.7 1.9 copy-done.5
  284.7 1.6 slice.120
  286.3 17.6 %rev.7 = f32[1,512,1024]{2,1,0:T(8,128)} reverse(f32[1,512,1024]{2,1,0:T(8,128)} %slice.120), dimensions={1,2} | reverse | bytes 4194304 | tf_op jit(solution)/shard_map/rev | solution.py:160
  303.9 3.5 %fusion.24 = bf16[1,512,1024]{2,1,0:T(8,128)(2,1)} fusion(f32[1,512,1024]{2,1,0:T(8,128)} %rev.7, f32[2,512,1024]{2,1,0:T(8,128)} %copy-done.5), kind=kLoop, calls=%fused_computation.45 | loop fusion | flops 1048576 | bytes 5242880 | tf_op jit(solution)/shard_map/convert_element_type | solution.py:161
  (76 shorter events, 3.8 us)
Async XLA Ops:
  6.5 271.0 %copy-start = (bf16[1024,1024]{1,0:T(8,128)(2,1)S(1)}, bf16[1024,1024]{1,0:T(8,128)(2,1)}, u32[]{:S(2)}) copy-start(bf16[1024,1024]{1,0:T(8,128)(2,1)} %param.29) | copy-start | bytes 6291460
  6.5 156.6 %all-gather.9.cloned.1.call-start = ((), (), s32[]{:S(2)}) async-start(), calls=%async_computation | async-start | bytes 4718592 | tf_op jit(solution)/shard_map/all_gather | solution.py:35
  8.4 1.0 copy-start.3
  9.4 8.4 %collective-permute-start.1 = (bf16[1,3,1024]{2,1,0:T(4,128)(2,1)S(1)}, bf16[1,3,1024]{2,1,0:T(4,128)(2,1)S(1)}, u32[]{:S(2)}, u32[]{:S(2)}) collective-permute-start(bf16[1,3,1024]{2,1,0:T(4,128)(2,1)S(1)} %get-tuple-element.314), channel_id=1, source_target_pairs={{2,0},{4,2},{6,4},{8,6},{10,8},{12,10},{14,12},{3,1},{5,3},{7,5},{... | collective-permute-start | bytes 18440 | tf_op jit(solution)/shard_map/ppermute | solution.py:26
  10.7 30.0 %collective-permute-start = (bf16[1,3,1024]{2,1,0:T(4,128)(2,1)S(1)}, bf16[1,3,1024]{2,1,0:T(4,128)(2,1)S(1)}, u32[]{:S(2)}, u32[]{:S(2)}) collective-permute-start(bf16[1,3,1024]{2,1,0:T(4,128)(2,1)S(1)} %get-tuple-element.313), channel_id=1, source_target_pairs={{0,2},{2,4},{4,6},{6,8},{8,10},{10,12},{12,14},{1,3},{3,5},{5,7},{... | collective-permute-start | bytes 18440 | tf_op jit(solution)/shard_map/ppermute | solution.py:23
  40.7 8.2 %copy-start.13 = (f32[1280]{0:T(1024)S(1)}, f32[1280]{0:T(1024)}, u32[]{:S(2)}) copy-start(f32[1280]{0:T(1024)} %param.24) | copy-start | bytes 15364
  48.9 3.7 %copy-start.1 = (f32[2,515,2304]{2,1,0:T(8,128)}, f32[2,515,2304]{2,1,0:T(8,128)S(1)}, u32[]{:S(2)}) copy-start(f32[2,515,2304]{2,1,0:T(8,128)S(1)} %fusion.12) | copy-start | bytes 28477444
  52.6 2.4 copy-start.4
  52.6 2.4 copy-start.7
  52.6 2.4 copy-start.15
  52.6 2.4 copy-start.17
  70.6 5.9 %copy-start.12 = (f32[2,2,256,16]{2,3,1,0:T(8,128)S(1)}, f32[2,2,256,16]{2,3,1,0:T(8,128)}, u32[]{:S(2)}) copy-start(f32[2,2,256,16]{2,3,1,0:T(8,128)} %get-tuple-element.316) | copy-start | bytes 196612
  70.7 11.0 %copy-start.14 = (f32[2,2,16]{2,1,0:T(2,128)S(1)}, f32[2,2,16]{2,1,0:T(2,128)}, u32[]{:S(2)}) copy-start(f32[2,2,16]{2,1,0:T(2,128)} %custom-call.2) | copy-start | bytes 772
  87.8 149.1 %all-gather.11.cloned.1.call-start = ((), (), s32[]{:S(2)}) async-start(), calls=%async_computation.1 | async-start | bytes 4718592 | tf_op jit(solution)/shard_map/all_gather | solution.py:35
  245.9 3.7 %copy-start.6 = (bf16[2,2,256,16,64]{2,4,3,1,0:T(8,128)(2,1)S(1)}, bf16[2,2,256,16,64]{2,4,3,1,0:T(8,128)(2,1)}, u32[]{:S(2)}) copy-start(bf16[2,2,256,16,64]{2,4,3,1,0:T(8,128)(2,1)} %copy.65) | copy-start | bytes 6291460
  245.9 3.7 %copy-start.8 = (f32[2,2,256,256]{3,2,1,0:T(8,128)S(1)}, f32[2,2,256,256]{3,2,1,0:T(8,128)}, u32[]{:S(2)}) copy-start(f32[2,2,256,256]{3,2,1,0:T(8,128)} %fusion.53) | copy-start | bytes 3145732
  245.9 3.7 %copy-start.9 = (f32[2,2,16,256]{3,2,1,0:T(8,128)S(1)}, f32[2,2,16,256]{3,2,1,0:T(8,128)}, u32[]{:S(2)}) copy-start(f32[2,2,16,256]{3,2,1,0:T(8,128)} %get-tuple-element.317) | copy-start | bytes 196612
  245.9 3.7 %copy-start.10 = (pred[256,256]{1,0:T(8,128)(4,1)S(1)}, pred[256,256]{1,0:T(8,128)(4,1)}, u32[]{:S(2)}) copy-start(pred[256,256]{1,0:T(8,128)(4,1)} %iota_compare_fusion) | copy-start | bytes 196612
  245.9 3.7 %copy-start.11 = (f32[2,2,256,16]{2,3,1,0:T(8,128)S(1)}, f32[2,2,256,16]{2,3,1,0:T(8,128)}, u32[]{:S(2)}) copy-start(f32[2,2,256,16]{2,3,1,0:T(8,128)} %get-tuple-element.315) | copy-start | bytes 196612
  245.9 3.7 %copy-start.18 = (f32[16]{0:T(128)S(1)}, f32[16]{0:T(128)}, u32[]{:S(2)}) copy-start(f32[16]{0:T(128)} %param.27) | copy-start | bytes 196
  272.5 5.1 %copy-start.2 = (f32[2,512,1024]{2,1,0:T(8,128)S(1)}, f32[2,512,1024]{2,1,0:T(8,128)}, u32[]{:S(2)}) copy-start(f32[2,512,1024]{2,1,0:T(8,128)} %reshape.126) | copy-start | bytes 12582916
  272.5 5.1 %copy-start.16 = (f32[1024]{0:T(1024)S(1)}, f32[1024]{0:T(1024)}, u32[]{:S(2)}) copy-start(f32[1024]{0:T(1024)} %param.28) | copy-start | bytes 12292
  282.7 2.0 copy-start.5
Sparse Core Ops, SparseCore 0:
  88.0 75.0 all-gather.8
  165.2 71.6 all-gather.10
where the time goes:
time: 319 us; the launch traced here: 314 us
  waiting for transfers between devices  110 us (34%)
  local copies, waits for them, and re-layouts  76 us (24%)
  other arithmetic  37.1 us (12%)
  blocking collectives  35.7 us (11%)
  matrix products  34 us (11%)
  between operations  13.8 us (4%)
  starting transfers between devices  6.81 us (2%)
    all_gather x2, waiting for transfers between devices, prefix(): gathered = jax.tree.map(lambda a: lax.all_gather(a, axis), part)  110 us
    all_gather x2, blocking collectives, prefix(): gathered = jax.tree.map(lambda a: lax.all_gather(a, axis), part)  35.7 us
    rev x1, local copies, waits for them, and re-layouts, on_device(): reverse_ext = extended_all[:, margin:][:, ::-1, ::-1]  20.6 us
    rev x1, local copies, waits for them, and re-layouts, on_device(): mixed = outputs[:slabs] + outputs[slabs:][:, ::-1, ::-1]  17.6 us
    reshape x2, local copies, waits for them, and re-layouts, normalize(): flat = scanned.reshape(count, -1, H * P_SIZE)  15.7 us
    reshape x2, local copies, waits for them, and re-layouts, local_terms(): heads_x = activated[:, :, :inner].reshape(count, spans, Q, H, P_SIZE)  12.2 us
    add x7, other arithmetic, chain_states(): next_decay[..., None, None] * first_state + next_state  8.31 us
    dot_general x1, matrix products, local_terms(): jnp.einsum('grd,de->gre', extended, w_in, preferred_element_type=jnp.floa...  8.19 us
  transfers between devices with their start and end apart: 4, of which 2 were waited for; matrix products, arithmetic and copies ran while one was open for 9% of the time, Pallas kernels for 0%

commit v1 on v0

v1 whole, which is shorter than its diff:
```python
import functools

import jax
import jax.numpy as jnp
from jax import lax
from jax.experimental import pallas as pl
from jax.experimental.pallas import tpu as pltpu
from jax.sharding import PartitionSpec as P

H = 16
P_SIZE = 64
N = 128
Q = 256
KCONV = 4
D = 1024
INNER = H * P_SIZE
CONV = INNER + 2 * N
LANES = 128
CHUNKS = 2
HEADS_C = H // 2 // CHUNKS
ROWS_C = HEADS_C * P_SIZE
EDGE = 8

norm_epsilon = 1e-05
F32 = jnp.float32
BF16 = jnp.bfloat16
MESH = pl.DeviceIdType.MESH


def dot(a, b):
    return jnp.dot(a, b, preferred_element_type=F32)


def silu(a):
    half = 0.5 * a
    return half * (1.0 + jnp.tanh(half))


def kernel(
    rows, strand_ref, w_in_ref, w_dt_ref, conv_w_ref, conv_b_ref, dt_bias_ref, a_log_ref, d_skip_ref,
    gain_ref, w_out_ref, out_ref,
    v, source, halo, act, gate, inside, step, cum, cum_t, step_t, span_state, flipped_out,
    pack, pair_in, chain_in, chain_out, back_out, incoming,
    halo_send, halo_recv, pair_send, pair_recv, chain_send, chain_recv, back_send, back_recv,
):
    n = lax.axis_size("seq")
    me = lax.axis_index("seq")
    pairs = n // 2
    place, side = me // 2, me % 2
    other = 1 - side
    partner = me + 1 - 2 * side
    spans = rows // Q

    barrier = pltpu.get_barrier_semaphore()
    for off in (-2, -1, 1, 2):
        there = me + off

        @pl.when((there >= 0) & (there < n))
        def _(there=there):
            pl.semaphore_signal(barrier, inc=1, device_id={"seq": there}, device_id_type=MESH)

    pl.semaphore_wait(barrier, jnp.minimum(me, 2) + jnp.minimum(n - 1 - me, 2))

    row_id = lax.broadcasted_iota(jnp.int32, (Q, Q), 0)
    col_id = lax.broadcasted_iota(jnp.int32, (Q, Q), 1)
    exchange = jnp.where(row_id + col_id == Q - 1, 1.0, 0.0).astype(BF16)

    blocks = D // Q
    v[0] = strand_ref[...]
    for j in range(blocks):
        taken = strand_ref[:, (blocks - 1 - j) * Q : (blocks - j) * Q]
        v[1, :, j * Q : (j + 1) * Q] = dot(taken, exchange).astype(BF16)

    def halo_copy(strand):
        edge = rows if strand == 0 else EDGE
        return pltpu.make_async_remote_copy(
            src_ref=source.at[strand, pl.ds(edge, EDGE), :],
            dst_ref=halo.at[strand],
            send_sem=halo_send.at[strand],
            recv_sem=halo_recv.at[strand],
            device_id={"seq": me + 1 - 2 * strand},
            device_id_type=MESH,
        )

    def is_there(index):
        return (index >= 0) & (index < n)

    for strand in range(2):

        def columns_of(j, _, strand=strand):
            w_at = pl.ds(pl.multiple_of(INNER + j * Q, Q), Q)
            to = pl.ds(pl.multiple_of(j * Q, Q), Q)
            source[strand, EDGE : EDGE + rows, to] = dot(v[strand], w_in_ref[:, w_at])
            return 0

        lax.fori_loop(0, CONV // Q, columns_of, 0)

        @pl.when(is_there(me + 1 - 2 * strand))
        def _(strand=strand):
            halo_copy(strand).start()

    rates = -jnp.exp(a_log_ref[...])
    for strand in range(2):
        pre = dot(v[strand], w_dt_ref[...]) + dt_bias_ref[...]
        soft = jnp.maximum(pre, 0.0) + jnp.log1p(jnp.exp(-jnp.abs(pre)))
        step[strand] = soft
        keep = row_id >= col_id if strand == 0 else row_id <= col_id
        tri = jnp.where(keep, 1.0, 0.0).astype(F32)
        for span in range(spans):
            at = slice(span * Q, (span + 1) * Q)
            block_step = soft[at]
            total = jnp.dot(
                tri, block_step * rates, preferred_element_type=F32, precision=lax.Precision.HIGHEST
            )
            cum[strand, at, :] = total
            cum_t[strand, span] = jnp.transpose(total)[:H]
            step_t[strand, span] = jnp.transpose(block_step)[:H]

    for strand in range(2):
        first = 0 if strand == 0 else EDGE + rows

        @pl.when(is_there(me - 1 + 2 * strand))
        def _(strand=strand, first=first):
            halo_copy(strand).wait_recv()
            source[strand, first : first + EDGE, :] = halo[strand]

        @pl.when(jnp.logical_not(is_there(me - 1 + 2 * strand)))
        def _(strand=strand, first=first):
            source[strand, first : first + EDGE, :] = jnp.zeros((EDGE, CONV), F32)

        @pl.when(is_there(me + 1 - 2 * strand))
        def _(strand=strand):
            halo_copy(strand).wait_send()

        def conv_of(j, _, strand=strand):
            lanes = pl.ds(pl.multiple_of(j * LANES, LANES), LANES)
            for cut in range(0, rows, Q):
                summed = jnp.broadcast_to(conv_b_ref[:, lanes], (Q, LANES))
                for tap in range(KCONV):
                    shift = tap - KCONV + 1 if strand == 0 else KCONV - 1 - tap
                    low = EDGE + cut + shift
                    summed = summed + conv_w_ref[tap : tap + 1, lanes] * source[strand, low : low + Q, lanes]
                act[strand, cut : cut + Q, lanes] = silu(summed).astype(BF16)
            return 0

        lax.fori_loop(0, CONV // LANES, conv_of, 0)

        totals = []
        for span in range(spans):
            at = slice(span * Q, (span + 1) * Q)
            here = cum[strand, at, :]
            end = here[Q - 1 : Q] if strand == 0 else here[0:1]
            to_end = jnp.exp(end - here) * step[strand, at, :]
            b_rows = act[strand, at, INNER : INNER + N].astype(F32)
            for two in range(H // 2):
                x_two = act[strand, at, two * LANES : (two + 1) * LANES]
                both = jnp.concatenate(
                    [(b_rows * to_end[:, h : h + 1]).astype(BF16) for h in (2 * two, 2 * two + 1)], axis=1
                )
                prod = lax.dot_general(x_two, both, (((0,), (0,)), ((), ())), preferred_element_type=F32)
                low = two * LANES
                span_state[strand, span, low : low + P_SIZE] = prod[:P_SIZE, :N]
                span_state[strand, span, low + P_SIZE : low + LANES] = prod[P_SIZE:, N:]
            totals.append(jnp.exp(end))
        order = range(spans) if strand == 0 else range(spans - 1, -1, -1)
        for head in range(H):
            half, inner = divmod(head, H // 2)
            chunk, slot = divmod(inner, HEADS_C)
            at = slice(head * P_SIZE, (head + 1) * P_SIZE)
            state = None
            for span in order:
                one = totals[span][:, head : head + 1]
                if state is None:
                    state, decay = span_state[strand, span, at], one
                else:
                    state, decay = one * state + span_state[strand, span, at], one * decay
            pack[strand, half, chunk, slot * P_SIZE : (slot + 1) * P_SIZE] = state
            pack[strand, half, chunk, ROWS_C + slot : ROWS_C + slot + 1] = jnp.broadcast_to(decay, (1, N))
        for chunk in range(CHUNKS):
            for slot in range(HEADS_C, 8):
                for half in range(2):
                    pack[strand, half, chunk, ROWS_C + slot : ROWS_C + slot + 1] = jnp.zeros((1, N), F32)
            pair_copy = pltpu.make_async_remote_copy(
                src_ref=pack.at[strand, other, chunk],
                dst_ref=pair_in.at[strand, chunk],
                send_sem=pair_send.at[strand, chunk],
                recv_sem=pair_recv.at[strand, chunk],
                device_id={"seq": partner},
                device_id_type=MESH,
            )
            pair_copy.start()

    for strand in range(2):

        def gate_of(j, _, strand=strand):
            at = pl.ds(pl.multiple_of(j * Q, Q), Q)
            gate[strand, :, at] = silu(dot(v[strand], w_in_ref[:, at]))
            return 0

        lax.fori_loop(0, INNER // Q, gate_of, 0)
    for j in range(blocks):
        taken = w_out_ref[:, (blocks - 1 - j) * Q : (blocks - j) * Q]
        flipped_out[:, j * Q : (j + 1) * Q] = dot(taken, exchange).astype(BF16)

    def pair_of(strand, chunk):
        return pltpu.make_async_remote_copy(
            src_ref=pack.at[strand, other, chunk],
            dst_ref=pair_in.at[strand, chunk],
            send_sem=pair_send.at[strand, chunk],
            recv_sem=pair_recv.at[strand, chunk],
            device_id={"seq": partner},
            device_id_type=MESH,
        )

    def chain_of(strand, chunk):
        return pltpu.make_async_remote_copy(
            src_ref=chain_out.at[strand, chunk],
            dst_ref=chain_in.at[strand, chunk],
            send_sem=chain_send.at[strand, chunk],
            recv_sem=chain_recv.at[strand, chunk],
            device_id={"seq": me + 2 - 4 * strand},
            device_id_type=MESH,
        )

    def back_of(strand, chunk):
        return pltpu.make_async_remote_copy(
            src_ref=back_out.at[strand, chunk],
            dst_ref=incoming.at[strand, side, chunk],
            send_sem=back_send.at[strand, chunk],
            recv_sem=back_recv.at[strand, chunk],
            device_id={"seq": partner},
            device_id_type=MESH,
        )

    def hand_on(strand):
        earliest = (place + strand * (pairs - 1 - 2 * place)) == 0
        latest = (place + strand * (pairs - 1 - 2 * place)) == pairs - 1
        leads = side == strand
        for chunk in range(CHUNKS):
            pair_of(strand, chunk).wait_recv()

            @pl.when(earliest)
            def _(chunk=chunk):
                chain_in[strand, chunk] = jnp.zeros((ROWS_C, N), F32)

            @pl.when(jnp.logical_not(earliest))
            def _(chunk=chunk):
                chain_of(strand, chunk).wait_recv()

            for slot in range(HEADS_C):
                at = slice(slot * P_SIZE, (slot + 1) * P_SIZE)
                row = slice(ROWS_C + slot, ROWS_C + slot + 1)
                before = chain_in[strand, chunk, at]
                own = pack[strand, side, chunk, at]
                theirs = pair_in[strand, chunk, at]
                d_own = pack[strand, side, chunk, row]
                d_theirs = pair_in[strand, chunk, row]
                after_own = d_own * before + own
                after_theirs = d_theirs * before + theirs
                chain_out[strand, chunk, at] = jnp.where(
                    leads, d_theirs * after_own + theirs, d_own * after_theirs + own
                )
                back_out[strand, chunk, at] = jnp.where(leads, after_own, before)
                incoming[strand, side, chunk, at] = jnp.where(leads, before, after_theirs)

            @pl.when(jnp.logical_not(latest))
            def _(chunk=chunk):
                chain_of(strand, chunk).start()

            back_of(strand, chunk).start()

    half_q = Q // 2
    low_lanes = lax.broadcasted_iota(jnp.int32, (half_q, LANES), 1) < P_SIZE

    def inside_of(strand):
        def one_span(span, _):
            base = pl.multiple_of(span * Q, Q)
            b_rows = act[strand, pl.ds(base, Q), INNER : INNER + N]
            for part in range(2):
                top = pl.multiple_of(base + part * half_q, half_q)
                c_rows = act[strand, pl.ds(top, half_q), INNER + N :]
                whole = part == (1 if strand == 0 else 0)
                low, high = (0, Q) if whole else ((0, half_q) if strand == 0 else (half_q, Q))
                scores = lax.dot_general(
                    c_rows, b_rows[low:high], (((1,), (1,)), ((), ())), preferred_element_type=F32
                )
                t_id = lax.broadcasted_iota(jnp.int32, scores.shape, 0) + part * half_q
                s_id = lax.broadcasted_iota(jnp.int32, scores.shape, 1) + low
                scores = jnp.where(t_id >= s_id if strand == 0 else t_id <= s_id, scores, 0.0)
                here = cum[strand, pl.ds(top, half_q), :]
                for two in range(H // 2):
                    x_two = act[
                        strand, pl.ds(pl.multiple_of(base + low, half_q), high - low), two * LANES : (two + 1) * LANES
                    ]
                    found = []
                    for h in (2 * two, 2 * two + 1):
                        gaps = here[:, h : h + 1] - cum_t[strand, span, h : h + 1, low:high]
                        decays = jnp.exp(jnp.minimum(gaps, 0.0))
                        weights = (decays * scores * step_t[strand, span, h : h + 1, low:high]).astype(BF16)
                        found.append(dot(weights, x_two))
                    inside[strand, pl.ds(top, half_q), two * LANES : (two + 1) * LANES] = jnp.where(
                        low_lanes, found[0], found[1]
                    )
            return 0

        lax.fori_loop(0, spans, one_span, 0)

    lead = jnp.where(place < pairs // 2, 0, 1)
    hand_on(lead)
    inside_of(0)
    hand_on(1 - lead)
    inside_of(1)


    for strand in range(2):
        for chunk in range(CHUNKS):
            back_of(strand, chunk).wait_recv()

    low_lanes_q = lax.broadcasted_iota(jnp.int32, (Q, LANES), 1) < P_SIZE
    for strand in range(2):
        order = range(spans) if strand == 0 else range(spans - 1, -1, -1)
        previous = None
        for span in order:
            at = slice(span * Q, (span + 1) * Q)
            here = cum[strand, at, :]
            if previous is not None:
                last = previous * Q + (Q - 1 if strand == 0 else 0)
                total = jnp.exp(cum[strand, last : last + 1, :])
                for head in range(H):
                    half, inner = divmod(head, H // 2)
                    chunk, slot = divmod(inner, HEADS_C)
                    rows_h = slice(slot * P_SIZE, (slot + 1) * P_SIZE)
                    all_h = slice(head * P_SIZE, (head + 1) * P_SIZE)
                    incoming[strand, half, chunk, rows_h] = (
                        total[:, head : head + 1] * incoming[strand, half, chunk, rows_h]
                        + span_state[strand, previous, all_h]
                    )
            c_rows = act[strand, at, INNER + N :]
            c_both = jnp.concatenate([c_rows, c_rows], axis=1)
            grown = jnp.exp(here)
            squares = jnp.zeros((Q, 1), F32)
            for half in range(2):
                for chunk in range(CHUNKS):
                    start = incoming[strand, half, chunk]
                    upper = start.astype(BF16)
                    lower = (start - upper.astype(F32)).astype(BF16)
                    carried = lax.dot_general(
                        c_both,
                        jnp.concatenate([upper, lower], axis=1),
                        (((1,), (1,)), ((), ())),
                        preferred_element_type=F32,
                    )
                    head0 = half * (H // 2) + chunk * HEADS_C
                    for pos in range(HEADS_C // 2):
                        h = head0 + 2 * pos
                        lanes = slice(h * P_SIZE, h * P_SIZE + LANES)
                        scale = jnp.where(low_lanes_q, grown[:, h : h + 1], grown[:, h + 1 : h + 2])
                        scanned = (
                            inside[strand, at, lanes]
                            + scale * carried[:, pos * LANES : (pos + 1) * LANES]
                            + d_skip_ref[:, lanes] * act[strand, at, lanes].astype(F32)
                        )
                        gated = scanned * gate[strand, at, lanes]
                        inside[strand, at, lanes] = gated
                        squares = squares + jnp.sum(gated * gated, axis=1, keepdims=True)
            scale = lax.rsqrt(squares * (1.0 / INNER) + norm_epsilon)
            v[strand, at, :] = (inside[strand, at, :] * scale * gain_ref[...]).astype(BF16)
            previous = span

    def out_of(j, _):
        at = pl.ds(pl.multiple_of(j * Q, Q), Q)
        out_ref[:, at] = (dot(v[0], w_out_ref[:, at]) + dot(v[1], flipped_out[:, at])).astype(BF16)
        return 0

    lax.fori_loop(0, D // Q, out_of, 0)

    for strand in range(2):
        leaves = me + 2 - 4 * strand
        for chunk in range(CHUNKS):
            pair_of(strand, chunk).wait_send()
            back_of(strand, chunk).wait_send()

            @pl.when(is_there(leaves))
            def _(strand=strand, chunk=chunk):
                chain_of(strand, chunk).wait_send()


def on_device(
    tokens, hidden, base_table, w_in, w_dt, conv_w, conv_b, dt_bias, a_log, d_skip, norm_gain, w_out
):
    rows = hidden.shape[1]
    spans = rows // Q
    one_hot = (tokens[:, :, None] == jnp.arange(4)[None, None, :]).astype(BF16)
    looked = jnp.einsum("gtb,bd->gtd", one_hot, base_table, preferred_element_type=F32)
    strand_input = (hidden.astype(F32) + looked).astype(BF16)[0]
    wide = ((0, 0), (0, LANES - H))
    dma = pltpu.SemaphoreType.DMA
    outputs = pl.pallas_call(
        functools.partial(kernel, rows),
        out_shape=jax.ShapeDtypeStruct((rows, D), BF16),
        in_specs=[pl.BlockSpec(memory_space=pltpu.VMEM)] * 10,
        out_specs=pl.BlockSpec(memory_space=pltpu.VMEM),
        scratch_shapes=[
            pltpu.VMEM((2, rows, D), BF16),
            pltpu.VMEM((2, rows + 2 * EDGE, CONV), F32),
            pltpu.VMEM((2, EDGE, CONV), F32),
            pltpu.VMEM((2, rows, CONV), BF16),
            pltpu.VMEM((2, rows, INNER), F32),
            pltpu.VMEM((2, rows, INNER), F32),
            pltpu.VMEM((2, rows, LANES), F32),
            pltpu.VMEM((2, rows, LANES), F32),
            pltpu.VMEM((2, spans, H, Q), F32),
            pltpu.VMEM((2, spans, H, Q), F32),
            pltpu.VMEM((2, spans, INNER, N), F32),
            pltpu.VMEM((INNER, D), BF16),
            pltpu.VMEM((2, 2, CHUNKS, ROWS_C + 8, N), F32),
            pltpu.VMEM((2, CHUNKS, ROWS_C + 8, N), F32),
            pltpu.VMEM((2, CHUNKS, ROWS_C, N), F32),
            pltpu.VMEM((2, CHUNKS, ROWS_C, N), F32),
            pltpu.VMEM((2, CHUNKS, ROWS_C, N), F32),
            pltpu.VMEM((2, 2, CHUNKS, ROWS_C, N), F32),
            dma((2,)),
            dma((2,)),
            dma((2, CHUNKS)),
            dma((2, CHUNKS)),
            dma((2, CHUNKS)),
            dma((2, CHUNKS)),
            dma((2, CHUNKS)),
            dma((2, CHUNKS)),
        ],
        compiler_params=pltpu.CompilerParams(
            collective_id=0, has_side_effects=True, vmem_limit_bytes=58 * 1024 * 1024
        ),
    )(
        strand_input,
        w_in,
        jnp.pad(w_dt, wide),
        conv_w,
        conv_b[None],
        jnp.pad(dt_bias[None], wide),
        jnp.pad(a_log[None], wide),
        jnp.repeat(d_skip, P_SIZE)[None],
        norm_gain[None],
        w_out,
    )
    return outputs[None]


def solution(mesh):
    placed = (P(("groups", "batch"), "seq"), P(("groups", "batch"), "seq", None)) + (P(),) * 10
    return jax.shard_map(
        on_device,
        mesh=mesh,
        in_specs=placed,
        out_specs=P(("groups", "batch"), "seq", None),
        check_vma=False,
    )
```

time: 319 us -> 72.7 us (0.23); the launches traced: 314 us -> 72.3 us
  waiting for transfers between devices: 110 us -> 0 us
  local copies, waits for them, and re-layouts: 76 us -> 9.01 us
  Pallas kernels: 0 us -> 60.6 us
  other arithmetic: 37.1 us -> 0 us
  blocking collectives: 35.7 us -> 0 us
  matrix products: 34 us -> 2.69 us
  between operations: 13.8 us -> 0.02 us
  starting transfers between devices: 6.81 us -> 0 us
    all_gather x2 -> x0, waiting for transfers between devices: 110 us -> none  [prefix(): gathered = jax.tree.map(lambda a: lax.all_gather(a, axis), part)]
    pallas_call x0 -> x1, Pallas kernels: none -> 60.6 us  [on_device(): pl.pallas_call(functools.partial(kernel, rows), out_shape=jax.ShapeDtypeS...]
    rev x2 -> x0, local copies, waits for them, and re-layouts: 38.2 us -> none  [the longest x1 20.6 us: on_device(): reverse_ext = extended_all[:, margin:][:, ::-1, ::-1]]
    all_gather x2 -> x0, blocking collectives: 35.7 us -> none  [prefix(): gathered = jax.tree.map(lambda a: lax.all_gather(a, axis), part)]
    dot_general x8 -> x1, matrix products: 34 us -> 2.69 us  [on_device(): jnp.einsum('gtb,bd->gtd', one_hot, base_table, preferred_element_type=F32)]
    reshape x5 -> x0, local copies, waits for them, and re-layouts: 27.9 us -> none  [the longest x2 15.7 us: normalize(): flat = scanned.reshape(count, -1, H * P_SIZE)]
    add x9 -> x0, other arithmetic: 11.1 us -> none  [the longest x7 8.31 us: chain_states(): next_decay[..., None, None] * first_state + next_state]
    convert_element_type x3 -> x0, other arithmetic: 8.69 us -> none  [the longest x1 3.51 us: on_device(): return mixed.astype(jnp.bfloat16)]
  transfers between devices with their start and end apart: 4 -> 0, of which waited for: 2 -> 0; matrix products, arithmetic and copies ran while one was open for 9% -> 0% of each run, Pallas kernels for 0% -> 0%
where the time goes in v1:
time: 72.7 us; the launch traced here: 72.3 us
  Pallas kernels  60.6 us (83%)
  local copies, waits for them, and re-layouts  9.01 us (12%)
  matrix products  2.69 us (4%)
    pallas_call x1, Pallas kernels, on_device(): pl.pallas_call(functools.partial(kernel, rows), out_shape=jax.ShapeDtypeS...  60.6 us
    unnamed x4, local copies, waits for them, and re-layouts  3.19 us
    dot_general x1, matrix products, on_device(): jnp.einsum('gtb,bd->gtd', one_hot, base_table, preferred_element_type=F32)  2.69 us

profile of v1, /device:TPU:0, one launch (start us, length us, event | category | flops | bytes accessed | tf_op | source)
XLA Modules:
  0.0 72.3 jit_solution(11953959262591877608)
XLA Ops:
  0.0 0.0 copy-start
  0.0 1.2 %pad.12.dt_bias_ref = f32[1,128]{1,0:T(1,128)} pad(f32[1,16]{1,0:T(1,128)} %bitcast.17, f32[]{:T(128)} %constant.4.clone.1), padding=0_0x0_112 | pad | bytes 580 | tf_op jit(solution)/shard_map/jit(_pad)/pad | solution.py:440
  1.2 1.2 %pad.13.a_log_ref = f32[1,128]{1,0:T(1,128)} pad(f32[1,16]{1,0:T(1,128)} %bitcast.18, f32[]{:T(128)} %constant.4.clone.1), padding=0_0x0_112 | pad | bytes 580 | tf_op jit(solution)/shard_map/jit(_pad)/pad | solution.py:441
  2.4 1.3 %broadcast_in_dim.20.conv_b_ref = f32[1,1280]{1,0:T(1,128)} reshape(f32[1280]{0:T(1024)} %param.18) | data formatting | bytes 10240 | tf_op jit(solution)/shard_map/broadcast_in_dim | solution.py:439
  3.7 0.7 %broadcast_in_dim.23 = f32[16,64]{1,0:T(8,128)S(1)} broadcast(f32[16]{0:T(128)} %param.21), dimensions={0} | broadcast | bytes 4160 | tf_op jit(solution)/shard_map/broadcast_in_dim | solution.py:442
  4.4 0.7 broadcast_in_dim_reshape.3.d_skip_ref
  5.1 0.9 %copy.13 = bf16[1024,16]{1,0:T(8,128)(2,1)S(1)} copy(bf16[1024,16]{0,1:T(8,128)(2,1)} %param.16) | data formatting | bytes 65536 | tf_op args[4]
  6.0 0.8 %pad.11.w_dt_ref = bf16[1024,128]{1,0:T(8,128)(2,1)} pad(bf16[1024,16]{1,0:T(8,128)(2,1)S(1)} %copy.13, bf16[]{:T(256)} %constant.3.clone.1), padding=0_0x0_112 | pad | bytes 294914 | tf_op jit(solution)/shard_map/jit(_pad)/pad | solution.py:437
  6.8 0.0 copy-done
  6.8 2.7 %fusion.1.strand_ref = bf16[512,1024]{1,0:T(8,128)(2,1)} fusion(bf16[4,1024]{1,0:T(4,128)(2,1)S(1)} %copy-done, bf16[1,512,1024]{2,1,0:T(8,128)(2,1)} %param.13, s32[512]{0:T(512)} %bitcast.16), kind=kOutput, calls=%fused_computation.2 | convolution fusion | flops 5769216 | bytes 2107392 | tf_op jit(solution)/shard_map/gtb,bd->gtd/dot_general | solution.py:394
  9.5 60.6 %shard_map.118 = bf16[512,1024]{1,0:T(8,128)(2,1)} custom-call(bf16[512,1024]{1,0:T(8,128)(2,1)} %fusion.1.strand_ref, bf16[1024,2304]{1,0:T(8,128)(2,1)} %w_in_ref.1, bf16[1024,128]{1,0:T(8,128)(2,1)} %pad.11.w_dt_ref, f32[4,1280]{1,0:T(4,128)} %conv_w_ref.1, f32[1,1280]{1,0:T(1,128)} %broadcast_in_dim.20.conv_b_ref, f32[1,128]{1,0:T(1,128)} %pad.12.dt_bias_ref, ...), custom_call_target="tpu_custom_call" | custom-call | tf_op jit(solution)/shard_map/pallas_call | solution.py:398
  70.1 2.3 %copy.15 = bf16[1,512,1024]{2,1,0:T(8,128)(2,1)} copy(bf16[1,512,1024]{2,1,0:T(8,128)(2,1)} %bitcast.14) | data formatting | bytes 2097152
Async XLA Ops:
  0.0 6.8 %copy-start = (bf16[4,1024]{1,0:T(4,128)(2,1)S(1)}, bf16[4,1024]{1,0:T(4,128)(2,1)}, u32[]{:S(2)}) copy-start(bf16[4,1024]{1,0:T(4,128)(2,1)} %param.14) | copy-start | bytes 24580

commit v2 on v1

--- a/solution.py
+++ b/solution.py
@@ -37,9 +37,9 @@
 
 
 def kernel(
-    rows, strand_ref, w_in_ref, w_dt_ref, conv_w_ref, conv_b_ref, dt_bias_ref, a_log_ref, d_skip_ref,
+    rows, tokens_ref, hidden_ref, table_ref, w_in_ref, w_dt_ref, conv_w_ref, conv_b_ref, dt_bias_ref, a_log_ref, d_skip_ref,
     gain_ref, w_out_ref, out_ref,
-    v, source, halo, act, gate, inside, step, cum, cum_t, step_t, span_state, flipped_out,
+    table, wide_dt, small, d_wide, v, source, halo, act, gate, inside, step, cum, cum_t, step_t, span_state, flipped_out,
     pack, pair_in, chain_in, chain_out, back_out, incoming,
     halo_send, halo_recv, pair_send, pair_recv, chain_send, chain_recv, back_send, back_recv,
 ):
@@ -66,9 +66,17 @@
     exchange = jnp.where(row_id + col_id == Q - 1, 1.0, 0.0).astype(BF16)
 
     blocks = D // Q
-    v[0] = strand_ref[...]
+    table[...] = jnp.zeros((EDGE, D), F32)
+    table[:4] = table_ref[...].astype(F32)
+    lookup = jnp.concatenate([table[...], jnp.zeros((EDGE, D), F32)], axis=0).astype(BF16)
+    base_id = lax.broadcasted_iota(jnp.int32, (2 * EDGE, rows), 0)
+    one_hot = jnp.where(base_id == tokens_ref[...], 1.0, 0.0).astype(BF16)
     for j in range(blocks):
-        taken = strand_ref[:, (blocks - 1 - j) * Q : (blocks - j) * Q]
+        at = slice(j * Q, (j + 1) * Q)
+        looked = lax.dot_general(one_hot, lookup[:, at], (((0,), (0,)), ((), ())), preferred_element_type=F32)
+        v[0, :, at] = (hidden_ref[0, :, at].astype(F32) + looked).astype(BF16)
+    for j in range(blocks):
+        taken = v[0, :, (blocks - 1 - j) * Q : (blocks - j) * Q]
         v[1, :, j * Q : (j + 1) * Q] = dot(taken, exchange).astype(BF16)
 
     def halo_copy(strand):
@@ -99,9 +107,22 @@
         def _(strand=strand):
             halo_copy(strand).start()
 
-    rates = -jnp.exp(a_log_ref[...])
-    for strand in range(2):
-        pre = dot(v[strand], w_dt_ref[...]) + dt_bias_ref[...]
+    wide_dt[...] = jnp.zeros((LANES, D), BF16)
+    wide_dt[:H] = w_dt_ref[...]
+    small[...] = jnp.zeros((EDGE, LANES), F32)
+    small[0:1, :H] = dt_bias_ref[...]
+    small[1:2, :H] = a_log_ref[...]
+    low_lanes_one = lax.broadcasted_iota(jnp.int32, (1, LANES), 1) < P_SIZE
+    skips = d_skip_ref[...]
+    for two in range(H // 2):
+        d_wide[:, two * LANES : (two + 1) * LANES] = jnp.where(
+            low_lanes_one, skips[:, 2 * two : 2 * two + 1], skips[:, 2 * two + 1 : 2 * two + 2]
+        )
+    rates = -jnp.exp(small[1:2])
+    for strand in range(2):
+        pre = lax.dot_general(
+            v[strand], wide_dt[...], (((1,), (1,)), ((), ())), preferred_element_type=F32
+        ) + small[0:1]
         soft = jnp.maximum(pre, 0.0) + jnp.log1p(jnp.exp(-jnp.abs(pre)))
         step[strand] = soft
         keep = row_id >= col_id if strand == 0 else row_id <= col_id
@@ -135,7 +156,7 @@
         def conv_of(j, _, strand=strand):
             lanes = pl.ds(pl.multiple_of(j * LANES, LANES), LANES)
             for cut in range(0, rows, Q):
-                summed = jnp.broadcast_to(conv_b_ref[:, lanes], (Q, LANES))
+                summed = jnp.broadcast_to(conv_b_ref[pl.ds(j, 1), :], (Q, LANES))
                 for tap in range(KCONV):
                     shift = tap - KCONV + 1 if strand == 0 else KCONV - 1 - tap
                     low = EDGE + cut + shift
@@ -358,7 +379,7 @@
                         scanned = (
                             inside[strand, at, lanes]
                             + scale * carried[:, pos * LANES : (pos + 1) * LANES]
-                            + d_skip_ref[:, lanes] * act[strand, at, lanes].astype(F32)
+                            + d_wide[:, lanes] * act[strand, at, lanes].astype(F32)
                         )
                         gated = scanned * gate[strand, at, lanes]
                         inside[strand, at, lanes] = gated
@@ -390,17 +411,17 @@
 ):
     rows = hidden.shape[1]
     spans = rows // Q
-    one_hot = (tokens[:, :, None] == jnp.arange(4)[None, None, :]).astype(BF16)
-    looked = jnp.einsum("gtb,bd->gtd", one_hot, base_table, preferred_element_type=F32)
-    strand_input = (hidden.astype(F32) + looked).astype(BF16)[0]
-    wide = ((0, 0), (0, LANES - H))
     dma = pltpu.SemaphoreType.DMA
     outputs = pl.pallas_call(
         functools.partial(kernel, rows),
         out_shape=jax.ShapeDtypeStruct((rows, D), BF16),
-        in_specs=[pl.BlockSpec(memory_space=pltpu.VMEM)] * 10,
+        in_specs=[pl.BlockSpec(memory_space=pltpu.VMEM)] * 12,
         out_specs=pl.BlockSpec(memory_space=pltpu.VMEM),
         scratch_shapes=[
+            pltpu.VMEM((EDGE, D), F32),
+            pltpu.VMEM((LANES, D), BF16),
+            pltpu.VMEM((EDGE, LANES), F32),
+            pltpu.VMEM((1, INNER), F32),
             pltpu.VMEM((2, rows, D), BF16),
             pltpu.VMEM((2, rows + 2 * EDGE, CONV), F32),
             pltpu.VMEM((2, EDGE, CONV), F32),
@@ -432,14 +453,16 @@
             collective_id=0, has_side_effects=True, vmem_limit_bytes=58 * 1024 * 1024
         ),
     )(
-        strand_input,
+        tokens,
+        hidden,
+        base_table,
         w_in,
-        jnp.pad(w_dt, wide),
+        w_dt.T,
         conv_w,
-        conv_b[None],
-        jnp.pad(dt_bias[None], wide),
-        jnp.pad(a_log[None], wide),
-        jnp.repeat(d_skip, P_SIZE)[None],
+        conv_b.reshape(CONV // LANES, LANES),
+        dt_bias[None],
+        a_log[None],
+        d_skip[None],
         norm_gain[None],
         w_out,
     )

time: 72.7 us -> 63.3 us (0.87)
  local copies, waits for them, and re-layouts: 9.01 us -> 2.26 us
  matrix products: 2.69 us -> 0 us
    pad x3 -> x0, local copies, waits for them, and re-layouts: 3.15 us -> none  [the longest x1 1.2 us: on_device(): jnp.pad(a_log[None], wide)]
    dot_general x1 -> x0, matrix products: 2.69 us -> none  [on_device(): jnp.einsum('gtb,bd->gtd', one_hot, base_table, preferred_element_type=F32)]
    broadcast_in_dim x2 -> x0, local copies, waits for them, and re-layouts: 2.01 us -> none  [the longest x1 1.29 us: on_device(): conv_b[None]]
    unnamed x4 -> x1, local copies, waits for them, and re-layouts: 3.19 us -> 2.26 us
where the time goes in v2:
time: 63.3 us; the launch traced here: 63.1 us
  Pallas kernels  60.8 us (96%)
  local copies, waits for them, and re-layouts  2.26 us (4%)
    pallas_call x1, Pallas kernels, on_device(): pl.pallas_call(functools.partial(kernel, rows), out_shape=jax.ShapeDtypeS...  60.8 us
    unnamed x1, local copies, waits for them, and re-layouts  2.26 us

profile of v2, /device:TPU:0, one launch (start us, length us, event | category | flops | bytes accessed | tf_op | source)
XLA Modules:
  0.0 63.1 jit_solution(6929921203022853724)
XLA Ops:
  0.0 60.8 %shard_map.118 = bf16[512,1024]{1,0:T(8,128)(2,1)} custom-call(s32[1,512]{1,0:T(1,128)} %tokens_ref.1, bf16[1,512,1024]{2,1,0:T(8,128)(2,1)} %hidden_ref.1, bf16[4,1024]{1,0:T(4,128)(2,1)} %table_ref.1, bf16[1024,2304]{1,0:T(8,128)(2,1)} %w_in_ref.1, bf16[16,1024]{1,0:T(8,128)(2,1)} %bitcast.8, f32[4,1280]{1,0:T(4,128)} %conv_w_ref.1, f32[10,128]{1,0:T(8,128)} %bitcast.9, ...), custom_call_target="tpu_custom_call" | custom-call | tf_op jit(solution)/shard_map/pallas_call | solution.py:415
  60.8 2.3 %copy.14 = bf16[1,512,1024]{2,1,0:T(8,128)(2,1)} copy(bf16[1,512,1024]{2,1,0:T(8,128)(2,1)} %bitcast.7) | data formatting | bytes 2097152

commit v3 on v2

--- a/solution.py
+++ b/solution.py
@@ -16,7 +16,7 @@
 INNER = H * P_SIZE
 CONV = INNER + 2 * N
 LANES = 128
-CHUNKS = 2
+CHUNKS = 4
 HEADS_C = H // 2 // CHUNKS
 ROWS_C = HEADS_C * P_SIZE
 EDGE = 8

time: 63.3 us -> 59.9 us (0.946)
  Pallas kernels: 60.8 us -> 57.5 us
    pallas_call x1, Pallas kernels: 60.8 us -> 57.5 us  [on_device(): pl.pallas_call(functools.partial(kernel, rows), out_shape=jax.ShapeDtypeS...]
where the time goes in v3:
time: 59.9 us; the launch traced here: 59.8 us
  Pallas kernels  57.5 us (96%)
  local copies, waits for them, and re-layouts  2.26 us (4%)
    pallas_call x1, Pallas kernels, on_device(): pl.pallas_call(functools.partial(kernel, rows), out_shape=jax.ShapeDtypeS...  57.5 us
    unnamed x1, local copies, waits for them, and re-layouts  2.26 us

profile of v3, /device:TPU:0, one launch (start us, length us, event | category | flops | bytes accessed | tf_op | source)
XLA Modules:
  0.0 59.8 jit_solution(7450799729152978194)
XLA Ops:
  0.0 57.5 %shard_map.118 = bf16[512,1024]{1,0:T(8,128)(2,1)} custom-call(s32[1,512]{1,0:T(1,128)} %tokens_ref.1, bf16[1,512,1024]{2,1,0:T(8,128)(2,1)} %hidden_ref.1, bf16[4,1024]{1,0:T(4,128)(2,1)} %table_ref.1, bf16[1024,2304]{1,0:T(8,128)(2,1)} %w_in_ref.1, bf16[16,1024]{1,0:T(8,128)(2,1)} %bitcast.8, f32[4,1280]{1,0:T(4,128)} %conv_w_ref.1, f32[10,128]{1,0:T(8,128)} %bitcast.9, ...), custom_call_target="tpu_custom_call" | custom-call | tf_op jit(solution)/shard_map/pallas_call | solution.py:415
  57.5 2.3 %copy.14 = bf16[1,512,1024]{2,1,0:T(8,128)(2,1)} copy(bf16[1,512,1024]{2,1,0:T(8,128)(2,1)} %bitcast.7) | data formatting | bytes 2097152
